TPU v7x, 32 devices: a whole 2x2x4 slice. The times are simulated.
32 devices in a mesh: dp: 2 (over x), branch: 4 (over z), seq: 4 (over y, core).
Axes of the slice: x: 2, y: 2, z: 4, core: 2. Of those that a mesh axis runs over, the one named last changes fastest.
Arguments:
- qkv: bfloat16 [4, 2, 896, 3, 1536], P('branch', 'dp', 'seq'), may hold values from -5.5 to 5.5, as said below
- grad_base: bfloat16 [2, 896, 2432], P('dp', ('branch', 'seq')), may hold values from -12 to 12
- w_out: bfloat16 [4, 1536, 2432], P('branch', 'seq'), may hold values from -0.15625 to 0.15625
- scale_level: int32 [2], P('dp'), may hold values from 0 to 7
- text_count: int32 [2], P('dp'), may hold values from 96 to 384, as said below
Outputs:
- qkv_grad: bfloat16 [4, 2, 896, 3, 1536], P('branch', 'dp', 'seq')
- w_out_grad: float32 [4, 2432, 1536], P('branch', 'dp', 'seq')
Inputs may be any that keep to these rules, and one draw needn't show every extreme that they name: `qkv`: the queries, keys and values are real numbers of order one. `text_count`: some sample has all 384 text slots live in every draw.
All inputs are finite; a program needn't handle non-finite values.
Results may differ from a plain program's by a relative error of at most 0.0064.
Values may be sent and summed in bfloat16 or wider, within the bound.
A program may use at most 64 MiB of HBM per device.

v0:
```python
import math

import jax
import jax.numpy as jnp
from jax import lax
from jax.sharding import PartitionSpec as P

DH = 64
LAT = 512
SCALE_LEVELS = 8


def head_grads(queries, keys_h, values_h, out_grad, key_valid):
    inv_root = 1.0 / math.sqrt(queries.shape[-1])
    scores = jnp.dot(queries, keys_h.T, preferred_element_type=jnp.float32) * inv_root
    scores = jnp.where(key_valid[None, :], scores, -jnp.inf)
    row_max = jnp.max(scores, axis=1, keepdims=True)
    powers = jnp.exp(scores - row_max)
    probs = powers / jnp.sum(powers, axis=1, keepdims=True)
    probs_b = probs.astype(jnp.bfloat16)
    attended = jnp.dot(probs_b, values_h, preferred_element_type=jnp.float32).astype(jnp.bfloat16)
    prob_grad = jnp.dot(out_grad, values_h.T, preferred_element_type=jnp.float32)
    row_dot = jnp.sum(probs * prob_grad, axis=1, keepdims=True)
    score_grad = (probs * (prob_grad - row_dot)).astype(jnp.bfloat16)
    query_grad = jnp.dot(score_grad, keys_h, preferred_element_type=jnp.float32) * inv_root
    key_grad = jnp.dot(score_grad.T, queries, preferred_element_type=jnp.float32) * inv_root
    value_grad = jnp.dot(probs_b.T, out_grad, preferred_element_type=jnp.float32)
    return (attended, query_grad, key_grad, value_grad)


def attend(activation, upstream, weight, factor, key_valid):
    token_count = activation.shape[0]
    feature_width = weight.shape[0]
    head_count = feature_width // DH
    out_grad = (
        jnp.einsum("sd,hd->sh", upstream, weight, preferred_element_type=jnp.float32) * factor
    ).astype(jnp.bfloat16)

    def split_heads(matrix):
        return matrix.reshape(token_count, head_count, DH).transpose(1, 0, 2)

    def join_heads(matrix):
        return matrix.transpose(1, 0, 2).reshape(token_count, feature_width)

    def one_head(pieces):
        return head_grads(pieces[0], pieces[1], pieces[2], pieces[3], key_valid)

    attended, query_grad, key_grad, value_grad = lax.map(
        one_head,
        (
            split_heads(activation[:, 0]),
            split_heads(activation[:, 1]),
            split_heads(activation[:, 2]),
            split_heads(out_grad),
        ),
    )
    act_grads = jnp.stack(
        [join_heads(query_grad), join_heads(key_grad), join_heads(value_grad)], axis=1
    ).astype(jnp.bfloat16)
    return (act_grads, join_heads(attended))


def body(qkv, grad_base, w_out, scale_level, text_count):
    branch_id = lax.axis_index("branch")
    levels = jnp.arange(SCALE_LEVELS)
    column = jnp.where(
        branch_id == 0, jnp.float32(1.0), (levels + 2 * branch_id).astype(jnp.float32) / 8.0
    )
    picked = (scale_level[:, None] == levels[None, :]).astype(jnp.float32)
    factor = jnp.sum(picked * column[None, :], axis=1)[0]
    gathered = lax.all_gather(grad_base, ("branch", "seq"), axis=1, tiled=True)
    upstream = gathered[0]
    heads_act = lax.all_to_all(qkv, "seq", split_axis=4, concat_axis=2, tiled=True)[0, 0]
    positions = jnp.arange(upstream.shape[0])
    key_valid = positions < LAT + text_count[0]
    act_grads, attended = attend(heads_act, upstream, w_out[0], factor, key_valid)
    returned = lax.all_to_all(act_grads[None, None], "seq", split_axis=2, concat_axis=4, tiled=True)
    weight_grad = lax.psum_scatter(
        jnp.einsum("sd,sh->dh", upstream, attended, preferred_element_type=jnp.float32) * factor,
        "dp",
        scatter_dimension=0,
        tiled=True,
    )
    return (returned, weight_grad[None])


def solution(mesh):
    in_specs = (
        P("branch", "dp", "seq", None, None),
        P("dp", ("branch", "seq"), None),
        P("branch", "seq", None),
        P("dp"),
        P("dp"),
    )
    out_specs = (P("branch", "dp", "seq", None, None), P("branch", "dp", "seq"))
    return jax.shard_map(body, mesh=mesh, in_specs=in_specs, out_specs=out_specs, check_vma=False)
```

profile of v0, /device:TPU:0, one launch (start us, length us, event | category | flops | bytes accessed | tf_op | source)
XLA Modules:
  0.0 241.1 jit_solution(13275351410685676673)
XLA Ops:
  7.9 5.6 %copy.31 = bf16[1,1,224,3,1536]{2,3,1,0,4:T(4,128)(2,1)} copy(bf16[1,1,224,3,1536]{4,2,3,1,0:T(8,128)(2,1)} %param.7) | data formatting | bytes 4128768 | tf_op args[0]
  13.5 4.6 %all-to-all-start = ((bf16[1,1,224,3,1536]{2,3,1,0,4:T(4,128)(2,1)}), bf16[1,1,224,3,1536]{2,3,1,0,4:T(4,128)(2,1)}, u32[]{:S(2)}, u32[]{:S(2)}) async-start(bf16[1,1,224,3,1536]{2,3,1,0,4:T(4,128)(2,1)} %copy.31), calls=%async_computation | async-start | bytes 6291456 | tf_op jit(solution)/shard_map/all_to_all | solution.py:73
  20.2 50.2 %all-to-all-done = bf16[1,1,224,3,1536]{2,3,1,0,4:T(4,128)(2,1)} async-done(((bf16[1,1,224,3,1536]{2,3,1,0,4:T(4,128)(2,1)}), bf16[1,1,224,3,1536]{2,3,1,0,4:T(4,128)(2,1)}, u32[]{:S(2)}, u32[]{:S(2)}) %all-to-all-start) | async-done | bytes 2064416 | tf_op jit(solution)/shard_map/all_to_all | solution.py:73
  70.4 5.9 %copy.45 = bf16[1,1,224,3,4,384]{5,4,2,3,1,0:T(4,128)(2,1)} copy(bf16[1,1,224,3,4,384]{2,3,5,4,1,0:T(4,128)(2,1)} %bitcast) | data formatting | bytes 4128768 | tf_op jit(solution)/shard_map/all_to_all | solution.py:73
  83.5 5.9 %fusion.50 = bf16[896,384]{0,1:T(8,128)(2,1)} fusion(bf16[1,384,2432]{2,1,0:T(8,128)(2,1)S(1)} %copy-done, bf16[1,896,2432]{2,1,0:T(8,128)(2,1)} %all-gather.2.cloned.1.call-done, f32[]{:T(128)} %fusion.55), kind=kOutput, calls=%fused_computation.54 | convolution fusion | flops 1674215424 | bytes 6914052 | tf_op jit(solution)/shard_map/sd,hd->sh/dot_general | solution.py:36
  89.4 2.4 copy.37
  91.8 73.3 %while.17 = (s32[]{:T(128)}, bf16[6,896,64]{1,2,0:T(8,128)(2,1)}, bf16[6,896,64]{1,2,0:T(8,128)(2,1)}, bf16[6,896,64]{1,2,0:T(8,128)(2,1)}, bf16[6,896,64]{1,2,0...) while((s32[]{:T(128)}, bf16[6,896,64]{1,2,0:T(8,128)(2,1)}, ...), condition=%wide.region_5.6_spmd.clone, body=%wide.region_1.5_spmd.clone.sunk | while | flops 640817408 | bytes 32515952 | solution.py:48
  93.2 2.7 %fusion.87 = bf16[6,896,64]{1,2,0:T(8,128)(2,1)} fusion(bf16[6,896,64]{1,2,0:T(8,128)(2,1)} %get-tuple-element.233, s32[]{:T(128)} %get-tuple-element.229, bf16[6,896,64]{2,1,0:T(8,128)(2,1)} %get-tuple-element.248, f32[896,896]{0,1:T(8,128)S(1)} %get-tuple-element.214, f32[896]{0:T(1024)S(1)} %fusion.83, f32[896]{0:T(1024)S(1)} %get-tuple-element.215, ...), kind=kOutput, calls=%fused_computation.15.clone.1 | convolution fusion | flops 106774528 | bytes 3679104 | tf_op jit(solution)/shard_map/while/body/eval_jaxpr/dot_general | solution.py:27
  95.9 2.3 multiply_reduce_fusion.2
  101.5 2.5 %fusion.84 = bf16[6,896,64]{1,2,0:T(8,128)(2,1)} fusion(bf16[6,896,64]{1,2,0:T(8,128)(2,1)} %get-tuple-element.230, s32[]{:T(128)} %get-tuple-element.229, bf16[6,896,64]{1,2,0:T(8,128)(2,1)} %get-tuple-element.247, f32[896,896]{0,1:T(8,128)S(1)} %get-tuple-element.214, f32[896]{0:T(1024)S(1)} %fusion.83, f32[896]{0:T(1024)S(1)} %get-tuple-element.215, ...), kind=kOutput, calls=%fused_computation.18.clone.1 | convolution fusion | flops 106831872 | bytes 3449728 | tf_op jit(solution)/shard_map/while/body/eval_jaxpr/dot_general | solution.py:21
  105.4 2.7 %fusion.87 = bf16[6,896,64]{1,2,0:T(8,128)(2,1)} fusion(bf16[6,896,64]{1,2,0:T(8,128)(2,1)} %get-tuple-element.233, s32[]{:T(128)} %get-tuple-element.229, bf16[6,896,64]{2,1,0:T(8,128)(2,1)} %get-tuple-element.248, f32[896,896]{0,1:T(8,128)S(1)} %get-tuple-element.214, f32[896]{0:T(1024)S(1)} %fusion.83, f32[896]{0:T(1024)S(1)} %get-tuple-element.215, ...), kind=kOutput, calls=%fused_computation.15.clone.1 | convolution fusion | flops 106774528 | bytes 3679104 | tf_op jit(solution)/shard_map/while/body/eval_jaxpr/dot_general | solution.py:27
  108.1 2.3 multiply_reduce_fusion.2
  113.7 2.5 %fusion.84 = bf16[6,896,64]{1,2,0:T(8,128)(2,1)} fusion(bf16[6,896,64]{1,2,0:T(8,128)(2,1)} %get-tuple-element.230, s32[]{:T(128)} %get-tuple-element.229, bf16[6,896,64]{1,2,0:T(8,128)(2,1)} %get-tuple-element.247, f32[896,896]{0,1:T(8,128)S(1)} %get-tuple-element.214, f32[896]{0:T(1024)S(1)} %fusion.83, f32[896]{0:T(1024)S(1)} %get-tuple-element.215, ...), kind=kOutput, calls=%fused_computation.18.clone.1 | convolution fusion | flops 106831872 | bytes 3449728 | tf_op jit(solution)/shard_map/while/body/eval_jaxpr/dot_general | solution.py:21
  117.6 2.8 %fusion.87 = bf16[6,896,64]{1,2,0:T(8,128)(2,1)} fusion(bf16[6,896,64]{1,2,0:T(8,128)(2,1)} %get-tuple-element.233, s32[]{:T(128)} %get-tuple-element.229, bf16[6,896,64]{2,1,0:T(8,128)(2,1)} %get-tuple-element.248, f32[896,896]{0,1:T(8,128)S(1)} %get-tuple-element.214, f32[896]{0:T(1024)S(1)} %fusion.83, f32[896]{0:T(1024)S(1)} %get-tuple-element.215, ...), kind=kOutput, calls=%fused_computation.15.clone.1 | convolution fusion | flops 106774528 | bytes 3679104 | tf_op jit(solution)/shard_map/while/body/eval_jaxpr/dot_general | solution.py:27
  120.4 2.2 multiply_reduce_fusion.2
  125.9 2.5 %fusion.84 = bf16[6,896,64]{1,2,0:T(8,128)(2,1)} fusion(bf16[6,896,64]{1,2,0:T(8,128)(2,1)} %get-tuple-element.230, s32[]{:T(128)} %get-tuple-element.229, bf16[6,896,64]{1,2,0:T(8,128)(2,1)} %get-tuple-element.247, f32[896,896]{0,1:T(8,128)S(1)} %get-tuple-element.214, f32[896]{0:T(1024)S(1)} %fusion.83, f32[896]{0:T(1024)S(1)} %get-tuple-element.215, ...), kind=kOutput, calls=%fused_computation.18.clone.1 | convolution fusion | flops 106831872 | bytes 3449728 | tf_op jit(solution)/shard_map/while/body/eval_jaxpr/dot_general | solution.py:21
  129.8 2.8 %fusion.87 = bf16[6,896,64]{1,2,0:T(8,128)(2,1)} fusion(bf16[6,896,64]{1,2,0:T(8,128)(2,1)} %get-tuple-element.233, s32[]{:T(128)} %get-tuple-element.229, bf16[6,896,64]{2,1,0:T(8,128)(2,1)} %get-tuple-element.248, f32[896,896]{0,1:T(8,128)S(1)} %get-tuple-element.214, f32[896]{0:T(1024)S(1)} %fusion.83, f32[896]{0:T(1024)S(1)} %get-tuple-element.215, ...), kind=kOutput, calls=%fused_computation.15.clone.1 | convolution fusion | flops 106774528 | bytes 3679104 | tf_op jit(solution)/shard_map/while/body/eval_jaxpr/dot_general | solution.py:27
  138.1 2.5 %fusion.84 = bf16[6,896,64]{1,2,0:T(8,128)(2,1)} fusion(bf16[6,896,64]{1,2,0:T(8,128)(2,1)} %get-tuple-element.230, s32[]{:T(128)} %get-tuple-element.229, bf16[6,896,64]{1,2,0:T(8,128)(2,1)} %get-tuple-element.247, f32[896,896]{0,1:T(8,128)S(1)} %get-tuple-element.214, f32[896]{0:T(1024)S(1)} %fusion.83, f32[896]{0:T(1024)S(1)} %get-tuple-element.215, ...), kind=kOutput, calls=%fused_computation.18.clone.1 | convolution fusion | flops 106831872 | bytes 3449728 | tf_op jit(solution)/shard_map/while/body/eval_jaxpr/dot_general | solution.py:21
  142.0 2.8 %fusion.87 = bf16[6,896,64]{1,2,0:T(8,128)(2,1)} fusion(bf16[6,896,64]{1,2,0:T(8,128)(2,1)} %get-tuple-element.233, s32[]{:T(128)} %get-tuple-element.229, bf16[6,896,64]{2,1,0:T(8,128)(2,1)} %get-tuple-element.248, f32[896,896]{0,1:T(8,128)S(1)} %get-tuple-element.214, f32[896]{0:T(1024)S(1)} %fusion.83, f32[896]{0:T(1024)S(1)} %get-tuple-element.215, ...), kind=kOutput, calls=%fused_computation.15.clone.1 | convolution fusion | flops 106774528 | bytes 3679104 | tf_op jit(solution)/shard_map/while/body/eval_jaxpr/dot_general | solution.py:27
  144.8 2.3 multiply_reduce_fusion.2
  150.4 2.5 %fusion.84 = bf16[6,896,64]{1,2,0:T(8,128)(2,1)} fusion(bf16[6,896,64]{1,2,0:T(8,128)(2,1)} %get-tuple-element.230, s32[]{:T(128)} %get-tuple-element.229, bf16[6,896,64]{1,2,0:T(8,128)(2,1)} %get-tuple-element.247, f32[896,896]{0,1:T(8,128)S(1)} %get-tuple-element.214, f32[896]{0:T(1024)S(1)} %fusion.83, f32[896]{0:T(1024)S(1)} %get-tuple-element.215, ...), kind=kOutput, calls=%fused_computation.18.clone.1 | convolution fusion | flops 106831872 | bytes 3449728 | tf_op jit(solution)/shard_map/while/body/eval_jaxpr/dot_general | solution.py:21
  154.3 2.7 %fusion.87 = bf16[6,896,64]{1,2,0:T(8,128)(2,1)} fusion(bf16[6,896,64]{1,2,0:T(8,128)(2,1)} %get-tuple-element.233, s32[]{:T(128)} %get-tuple-element.229, bf16[6,896,64]{2,1,0:T(8,128)(2,1)} %get-tuple-element.248, f32[896,896]{0,1:T(8,128)S(1)} %get-tuple-element.214, f32[896]{0:T(1024)S(1)} %fusion.83, f32[896]{0:T(1024)S(1)} %get-tuple-element.215, ...), kind=kOutput, calls=%fused_computation.15.clone.1 | convolution fusion | flops 106774528 | bytes 3679104 | tf_op jit(solution)/shard_map/while/body/eval_jaxpr/dot_general | solution.py:27
  157.0 2.3 multiply_reduce_fusion.2
  162.6 2.5 %fusion.84 = bf16[6,896,64]{1,2,0:T(8,128)(2,1)} fusion(bf16[6,896,64]{1,2,0:T(8,128)(2,1)} %get-tuple-element.230, s32[]{:T(128)} %get-tuple-element.229, bf16[6,896,64]{1,2,0:T(8,128)(2,1)} %get-tuple-element.247, f32[896,896]{0,1:T(8,128)S(1)} %get-tuple-element.214, f32[896]{0:T(1024)S(1)} %fusion.83, f32[896]{0:T(1024)S(1)} %get-tuple-element.215, ...), kind=kOutput, calls=%fused_computation.18.clone.1 | convolution fusion | flops 106831872 | bytes 3449728 | tf_op jit(solution)/shard_map/while/body/eval_jaxpr/dot_general | solution.py:21
  165.1 7.1 %fusion.40 = f32[2432,384]{0,1:T(8,128)} fusion(bf16[896,384]{0,1:T(8,128)(2,1)} %bitcast.24, bf16[1,896,2432]{2,1,0:T(8,128)(2,1)} %all-gather.2.cloned.1.call-done, f32[]{:T(128)} %fusion.55), kind=kOutput, calls=%fused_computation.47 | convolution fusion | flops 1674461184 | bytes 8781828 | tf_op jit(solution)/shard_map/sd,sh->dh/dot_general | solution.py:79
  172.1 5.4 %copy.46 = f32[2432,384]{1,0:T(8,128)} copy(f32[2432,384]{0,1:T(8,128)} %fusion.40) | data formatting | bytes 7471104
  178.9 2.7 %pad_maximum_fusion = bf16[1,1,896,3,384]{2,4,3,1,0:T(8,128)(2,1)} fusion(bf16[1,1,896,1,384]{2,4,3,1,0:T(8,128)(2,1)} %bitcast.147, bf16[1,1,896,1,384]{2,4,3,1,0:T(8,128)(2,1)S(1)} %bitcast.146, bf16[1,1,896,1,384]{2,4,3,1,0:T(8,128)(2,1)S(1)} %bitcast.145), kind=kLoop, calls=%fused_computation.51 | loop fusion | flops 2064384 | bytes 4128768 | tf_op jit(solution)/shard_map/stack | solution.py:57
  181.5 5.8 %copy.41 = bf16[1,1,896,3,384]{4,3,1,0,2:T(4,128)(2,1)} copy(bf16[1,1,896,3,384]{2,4,3,1,0:T(8,128)(2,1)} %pad_maximum_fusion) | data formatting | bytes 4128768 | tf_op jit(solution)/shard_map/stack | solution.py:57
  187.3 36.4 %all_to_all.33 = bf16[1,1,896,3,384]{4,3,1,0,2:T(4,128)(2,1)S(1)} all-to-all(bf16[1,1,896,3,384]{4,3,1,0,2:T(4,128)(2,1)} %copy.41), channel_id=1, replica_groups=mesh['dp'=2,'branch'=4,'seq'=4] {'seq'}, dimensions={2} | all-to-all | bytes 4128768 | tf_op jit(solution)/shard_map/all_to_all | solution.py:77
  225.5 3.1 %reduce-scatter.4.cloned.1.call-done = f32[1216,384]{1,0:T(8,128)} async-done(((f32[2432,384]{1,0:T(8,128)}), f32[1216,384]{1,0:T(8,128)}) %reduce-scatter.4.cloned.1.call-update) | async-done | bytes 1867792
  228.6 2.9 %copy.47 = f32[1216,384]{0,1:T(8,128)} copy(f32[1216,384]{1,0:T(8,128)} %reduce-scatter.4.cloned.1.call-done) | data formatting | bytes 3735552
  231.5 2.8 %copy.44 = f32[1,1216,384]{2,1,0:T(8,128)} copy(f32[1,1216,384]{1,2,0:T(8,128)} %bitcast.138) | data formatting | bytes 3735552
  (60 shorter events, 42.1 us)
Async XLA Ops:
  7.2 76.3 %copy-start = (bf16[1,384,2432]{2,1,0:T(8,128)(2,1)S(1)}, bf16[1,384,2432]{2,1,0:T(8,128)(2,1)}, u32[]{:S(2)}) copy-start(bf16[1,384,2432]{2,1,0:T(8,128)(2,1)} %param.9) | copy-start | bytes 5603332
  7.2 76.3 %all-gather.2.cloned.1.call-start = ((), (), s32[]{:S(2)}) async-start(), calls=%async_computation.3 | async-start | bytes 4630528 | tf_op jit(solution)/shard_map/all_gather | solution.py:71
  13.5 56.9 %all-to-all-start = ((bf16[1,1,224,3,1536]{2,3,1,0,4:T(4,128)(2,1)}), bf16[1,1,224,3,1536]{2,3,1,0,4:T(4,128)(2,1)}, u32[]{:S(2)}, u32[]{:S(2)}) async-start(bf16[1,1,224,3,1536]{2,3,1,0,4:T(4,128)(2,1)} %copy.31), calls=%async_computation | async-start | bytes 6291456 | tf_op jit(solution)/shard_map/all_to_all | solution.py:73
  18.2 210.4 %reduce-scatter.4.cloned.1.call-start = ((), (), s32[]{:S(2)}) async-start(), calls=%async_computation.4 | async-start | bytes 5603328
  177.6 1.1 copy-start.1
  177.6 1.3 copy-start.2
Sparse Core Ops, SparseCore 0:
  10.2 68.3 all-gather.1
  177.7 50.8 reduce-scatter.3
where the time goes:
time: 243 us; the launch traced here: 241 us
  matrix products  75.9 us (31%)
  waiting for transfers between devices  54 us (22%)
  local copies, waits for them, and re-layouts  41.1 us (17%)
  blocking collectives  36.4 us (15%)
  between operations  15.4 us (6%)
  other arithmetic  13.6 us (6%)
  starting transfers between devices  4.72 us (2%)
    all_to_all x1, waiting for transfers between devices, body(): lax.all_to_all(qkv, 'seq', split_axis=4, concat_axis=2, tiled=True)[0, 0]  50.2 us
    all_to_all x1, blocking collectives, body(): lax.all_to_all(act_grads[None, None], 'seq', split_axis=2, concat_axis=4,...  36.4 us
    unnamed x10, local copies, waits for them, and re-layouts  18 us
    dot_general x6, matrix products, head_grads(): jnp.dot(probs_b.T, out_grad, preferred_element_type=jnp.float32)  16.5 us
    dot_general x6, matrix products, head_grads(): jnp.dot(probs_b, values_h, preferred_element_type=jnp.float32)  15.1 us
    dot_general x6, matrix products, head_grads(): jnp.dot(out_grad, values_h.T, preferred_element_type=jnp.float32)  13.5 us
    all_to_all x2, local copies, waits for them, and re-layouts, body(): lax.all_to_all(qkv, 'seq', split_axis=4, concat_axis=2, tiled=True)[0, 0]  7.77 us
    dot_general x6, matrix products, head_grads(): jnp.dot(score_grad.T, queries, preferred_element_type=jnp.float32)  7.7 us
  transfers between devices with their start and end apart: 3, of which 2 were waited for; matrix products, arithmetic and copies ran while one was open for 12% of the time, Pallas kernels for 0%

commit v1 on v0

v1 whole, which is shorter than its diff:
```python
import functools

import jax
import jax.numpy as jnp
from jax import lax
from jax.experimental import pallas as pl
from jax.experimental.pallas import tpu as pltpu
from jax.sharding import PartitionSpec as P

LAT = 512
MIN_TEXT = 96
F32 = jnp.float32
BF16 = jnp.bfloat16
MESH = pl.DeviceIdType.MESH
NT = (((1,), (1,)), ((), ()))
W = 128


def block_diag(pair):
    row = lax.broadcasted_iota(jnp.int32, pair.shape, 0)
    top = row < 64
    zero = jnp.zeros_like(pair)
    return jnp.concatenate([jnp.where(top, pair, zero), jnp.where(top, zero, pair)], axis=1)


def fold_diag(wide):
    row = lax.broadcasted_iota(jnp.int32, (wide.shape[0], W), 0)
    return jnp.where(row < 64, wide[:, :W], wide[:, W:])


def kernel(
    dp, seq, branch, chunks, tokens,
    x_ref, gb_ref, w_ref, level_ref, count_ref,
    out_ref, wg_ref,
    inb, slots, upc, dot_s, e_s, att32, inv_s, attb, q_t, k_t, v_t, gbuf, acc, partf, part_b, rbuf,
    qs, qr, rs, rr, zs, zr, ys, yr, cs, cr, fs, fr, ds_, dr, own_q, own_r,
):
    me_dp = lax.axis_index("dp")
    me_b = lax.axis_index("branch")
    me = lax.axis_index("seq")
    part = tokens // seq
    width = chunks * W
    nblk = tokens // W
    across = lax.rem(me + 2, seq)
    beside = me + 1 - 2 * lax.rem(me, 2)

    barrier = pltpu.get_barrier_semaphore()
    for d in range(1, branch):
        pl.semaphore_signal(barrier, inc=1, device_id={"branch": lax.rem(me_b + d, branch)}, device_id_type=MESH)
    for d in range(1, seq):
        pl.semaphore_signal(barrier, inc=1, device_id={"seq": lax.rem(me + d, seq)}, device_id_type=MESH)
    for d in range(1, dp):
        pl.semaphore_signal(barrier, inc=1, device_id={"dp": lax.rem(me_dp + d, dp)}, device_id_type=MESH)

    own = me_b * seq + me
    rows = gb_ref.shape[0]
    pad = slots.shape[1]
    mine = jnp.concatenate(
        [gb_ref[...].astype(F32), jnp.zeros((pad - rows, gb_ref.shape[1]), F32)], axis=0
    ).astype(BF16)
    slots[own] = mine
    pl.semaphore_wait(barrier, branch + seq + dp - 3)

    def remote(src, dst, ssem, rsem, axis, index):
        return pltpu.make_async_remote_copy(
            src_ref=src, dst_ref=dst, send_sem=ssem, recv_sem=rsem,
            device_id={axis: index}, device_id_type=MESH,
        )

    def qkv_copy(c, d):
        to = lax.rem(me + d, seq)
        lanes = pl.ds(pl.multiple_of(to * width + c * W, W), W)
        at = pl.ds(pl.multiple_of(me * part, 16), part)
        return remote(x_ref.at[:, :, lanes], inb.at[c, :, at, :], qs.at[c, d - 1], qr.at[c, d - 1], "seq", to)

    def qkv_own(c):
        lanes = pl.ds(pl.multiple_of(me * width + c * W, W), W)
        at = pl.ds(pl.multiple_of(me * part, 16), part)
        return pltpu.make_async_copy(x_ref.at[:, :, lanes], inb.at[c, :, at, :], own_q.at[c])

    def line(d):
        return lax.rem(me_b - d + branch, branch) * seq + me

    def z_copy(d):
        return remote(slots.at[own], slots.at[own], zs.at[d - 1], zr.at[d - 1], "branch", lax.rem(me_b + d, branch))

    def y_copy(d):
        return remote(slots.at[line(d)], slots.at[line(d)], ys.at[d], yr.at[d], "seq", across)

    def c_copy(d):
        return remote(slots.at[line(d)], slots.at[line(d)], cs.at[d], cr.at[d], "seq", beside)

    def f_copy(d):
        k = lax.rem(me_b - d + branch, branch) * seq + across
        return remote(slots.at[k], slots.at[k], fs.at[d], fr.at[d], "seq", beside)

    def ret_copy(c, d):
        to = lax.rem(me + d, seq)
        lanes = pl.ds(pl.multiple_of(me * width + c * W, W), W)
        at = pl.ds(pl.multiple_of(to * part, 16), part)
        return remote(gbuf.at[c, :, at, :], out_ref.at[:, :, lanes], rs.at[c, d - 1], rr.at[c, d - 1], "seq", to)

    def ret_own(c):
        lanes = pl.ds(pl.multiple_of(me * width + c * W, W), W)
        at = pl.ds(pl.multiple_of(me * part, 16), part)
        return pltpu.make_async_copy(gbuf.at[c, :, at, :], out_ref.at[:, :, lanes], own_r.at[c])

    def dp_copy(d):
        return remote(part_b.at[d - 1], rbuf.at[d - 1], ds_.at[d - 1], dr.at[d - 1], "dp", lax.rem(me_dp + d, dp))

    def send_qkv(c):
        for d in (2, 1, 3):
            qkv_copy(c, d).start()
        qkv_own(c).start()

    for d in range(1, branch):
        z_copy(d).start()
    send_qkv(0)
    y_copy(0).start()
    c_copy(0).start()
    send_qkv(1)
    send_qkv(2)

    level = level_ref[0]
    limit = LAT + count_ref[0]
    factor = jnp.where(me_b == 0, jnp.float32(1.0), (level + 2 * me_b).astype(F32) / 8.0)
    safe = LAT + MIN_TEXT
    tail = safe + lax.broadcasted_iota(jnp.int32, (tokens - safe, 2 * W), 0)

    def forward(c):
        for d in range(1, seq):
            qkv_copy(c, d).wait_recv()
        qkv_own(c).wait()
        q_t[c] = (inb[c, 0].astype(F32) * 0.125).T.astype(BF16)
        k_t[c] = inb[c, 1].astype(F32).T.astype(BF16)
        v_t[c] = inb[c, 2].astype(F32).T.astype(BF16)

        def step(i, carry):
            lanes = pl.ds(pl.multiple_of(i * W, W), W)
            wide = pl.ds(pl.multiple_of(i * 2 * W, 2 * W), 2 * W)
            s = jnp.dot(inb[c, 1], block_diag(q_t[c, :, lanes]), preferred_element_type=F32)
            s = jnp.concatenate([s[:safe], jnp.where(tail < limit, s[safe:], -1e30)], axis=0)
            top = jnp.max(s, axis=0, keepdims=True)
            e = jnp.exp(s - top)
            inv = 1.0 / jnp.sum(e, axis=0, keepdims=True)
            eb = e.astype(BF16)
            e_s[c, :, wide] = eb
            o = fold_diag(jnp.dot(v_t[c], eb, preferred_element_type=F32) * inv)
            att32[c, :, lanes] = o
            attb[pl.ds(c * W, W), lanes] = o.astype(BF16)
            inv_s[c, :, lanes] = fold_diag(jnp.broadcast_to(inv, (W, 2 * W)))
            return carry

        lax.fori_loop(0, nblk, step, 0)

    def backward(c):
        acc[...] = jnp.zeros_like(acc)

        def step(i, carry):
            lanes = pl.ds(pl.multiple_of(i * W, W), W)
            wide = pl.ds(pl.multiple_of(i * 2 * W, 2 * W), 2 * W)
            do = (dot_s[pl.ds(c * W, W), lanes] * inv_s[c, :, lanes]).astype(BF16)
            prod = do.astype(F32) * att32[c, :, lanes]
            delta = jnp.concatenate(
                [jnp.sum(prod[:64], axis=0, keepdims=True), jnp.sum(prod[64:], axis=0, keepdims=True)], axis=1
            )
            bd = block_diag(do)
            dpr = jnp.dot(inb[c, 2], bd, preferred_element_type=F32)
            eb = e_s[c, :, wide]
            ds = (eb.astype(F32) * (dpr - delta)).astype(BF16)
            acc[1] += lax.dot_general(eb, bd, NT, preferred_element_type=F32)
            acc[0] += lax.dot_general(ds, block_diag(q_t[c, :, lanes]), NT, preferred_element_type=F32)
            dq = fold_diag(jnp.dot(k_t[c], ds, preferred_element_type=F32)) * 0.125
            gbuf[c, 0, lanes, :] = dq.T.astype(BF16)
            return carry

        lax.fori_loop(0, nblk, step, 0)
        gbuf[c, 1] = acc[0].astype(BF16)
        gbuf[c, 2] = acc[1].astype(BF16)
        for d in (2, 1, 3):
            ret_copy(c, d).start()
        ret_own(c).start()

    def relay(d):
        z_copy(d).wait_recv()
        y_copy(d).start()
        c_copy(d).start()

    forward(0)
    for d in range(1, branch):
        relay(d)
    y_copy(0).wait_recv()
    f_copy(0).start()
    forward(1)
    for d in range(1, branch):
        y_copy(d).wait_recv()
        f_copy(d).start()
    forward(2)
    for d in range(branch):
        c_copy(d).wait_recv()
        f_copy(d).wait_recv()

    for b in range(branch):
        whole = jnp.concatenate([slots[b * seq + j].astype(F32)[:rows] for j in range(seq)], axis=0)
        upc[b * seq * rows:(b + 1) * seq * rows, :] = whole.astype(BF16)

    for at in range(0, tokens, 2 * W):
        size = min(2 * W, tokens - at)
        dot_s[:, at:at + size] = factor * lax.dot_general(
            w_ref[...], upc[at:at + size, :], NT, preferred_element_type=F32
        )

    backward(0)

    def weight_step(j, carry):
        lanes = pl.ds(pl.multiple_of(j * W, W), W)
        r = jnp.dot(attb[...], upc[:, lanes], preferred_element_type=F32)
        partf[lanes, :] = r.T * factor
        return carry

    lax.fori_loop(0, upc.shape[1] // W, weight_step, 0)
    share = wg_ref.shape[0]
    for d in range(1, dp):
        to = lax.rem(me_dp + d, dp)
        part_b[d - 1] = partf[pl.ds(pl.multiple_of(to * share, 8), share), :].astype(BF16)
        dp_copy(d).start()

    for c in range(1, chunks):
        backward(c)

    total = partf[pl.ds(pl.multiple_of(me_dp * share, 8), share), :]
    for d in range(1, dp):
        dp_copy(d).wait_recv()
        total = total + rbuf[d - 1].astype(F32)
    wg_ref[...] = total

    for c in range(chunks):
        ret_own(c).wait()
        for d in range(1, seq):
            ret_copy(c, d).wait_recv()
            ret_copy(c, d).wait_send()
            qkv_copy(c, d).wait_send()
    for d in range(1, branch):
        z_copy(d).wait_send()
    for d in range(branch):
        y_copy(d).wait_send()
        c_copy(d).wait_send()
        f_copy(d).wait_send()
    for d in range(1, dp):
        dp_copy(d).wait_send()


def body(dp, seq, branch, qkv, grad_base, w_out, scale_level, text_count):
    part, _, features = qkv.shape[2:]
    tokens = part * seq
    width = features // seq
    chunks = width // W
    rows, model = grad_base.shape[1:]
    pad = -(-rows // 16) * 16
    share = model // dp
    dma = pltpu.SemaphoreType.DMA
    vm = pltpu.VMEM
    vspec = pl.BlockSpec(memory_space=pltpu.VMEM)
    sspec = pl.BlockSpec(memory_space=pltpu.SMEM)
    anyspec = pl.BlockSpec(memory_space=pl.ANY)
    grads, weight_grad = pl.pallas_call(
        functools.partial(kernel, dp, seq, branch, chunks, tokens),
        out_shape=(
            jax.ShapeDtypeStruct((3, part, features), BF16),
            jax.ShapeDtypeStruct((share, width), F32),
        ),
        in_specs=[anyspec, vspec, vspec, sspec, sspec],
        out_specs=(anyspec, vspec),
        scratch_shapes=[
            vm((chunks, 3, tokens, W), BF16),
            vm((branch * seq, pad, model), BF16),
            vm((tokens, model), BF16),
            vm((width, tokens), F32),
            vm((chunks, tokens, 2 * tokens), BF16),
            vm((chunks, W, tokens), F32),
            vm((chunks, W, tokens), F32),
            vm((width, tokens), BF16),
            vm((chunks, W, tokens), BF16),
            vm((chunks, W, tokens), BF16),
            vm((chunks, W, tokens), BF16),
            vm((chunks, 3, tokens, W), BF16),
            vm((2, tokens, W), F32),
            vm((model, width), F32),
            vm((dp - 1, share, width), BF16),
            vm((dp - 1, share, width), BF16),
            dma((chunks, seq - 1)), dma((chunks, seq - 1)),
            dma((chunks, seq - 1)), dma((chunks, seq - 1)),
            dma((branch - 1,)), dma((branch - 1,)),
            dma((branch,)), dma((branch,)),
            dma((branch,)), dma((branch,)),
            dma((branch,)), dma((branch,)),
            dma((dp - 1,)), dma((dp - 1,)),
            dma((chunks,)), dma((chunks,)),
        ],
        compiler_params=pltpu.CompilerParams(
            collective_id=0, has_side_effects=True, vmem_limit_bytes=58 * 1024 * 1024
        ),
    )(jnp.transpose(qkv[0, 0], (1, 0, 2)), grad_base[0], w_out[0], scale_level, text_count)
    return (jnp.transpose(grads, (1, 0, 2))[None, None], weight_grad[None])


def solution(mesh):
    sizes = mesh.shape
    in_specs = (
        P("branch", "dp", "seq", None, None),
        P("dp", ("branch", "seq"), None),
        P("branch", "seq", None),
        P("dp"),
        P("dp"),
    )
    out_specs = (P("branch", "dp", "seq", None, None), P("branch", "dp", "seq"))
    run = functools.partial(body, sizes["dp"], sizes["seq"], sizes["branch"])
    return jax.shard_map(run, mesh=mesh, in_specs=in_specs, out_specs=out_specs, check_vma=False)
```

time: 243 us -> 108 us (0.44)
  Pallas kernels: 0 us -> 102 us
  matrix products: 75.9 us -> 0 us
  waiting for transfers between devices: 54 us -> 0 us
  local copies, waits for them, and re-layouts: 41.1 us -> 4.4 us
  blocking collectives: 36.4 us -> 0 us
  other arithmetic: 13.6 us -> 0 us
  between operations: 15.4 us -> 1.94 us
  starting transfers between devices: 4.72 us -> 0 us
    pallas_call x0 -> x1, Pallas kernels: none -> 102 us  [body(): pl.pallas_call(functools.partial(kernel, dp, seq, branch, chunks, tokens)...]
    dot_general x38 -> x0, matrix products: 75.9 us -> none  [the longest x6 16.5 us: head_grads(): jnp.dot(probs_b.T, out_grad, preferred_element_type=jnp.float32)]
    all_to_all x1 -> x0, waiting for transfers between devices: 50.2 us -> none  [body(): lax.all_to_all(qkv, 'seq', split_axis=4, concat_axis=2, tiled=True)[0, 0]]
    all_to_all x1 -> x0, blocking collectives: 36.4 us -> none  [body(): lax.all_to_all(act_grads[None, None], 'seq', split_axis=2, concat_axis=4,...]
    unnamed x10 -> x4, local copies, waits for them, and re-layouts: 18 us -> 4.4 us
    all_to_all x4 -> x0, local copies, waits for them, and re-layouts: 9.6 us -> none  [the longest x2 7.77 us: body(): lax.all_to_all(qkv, 'seq', split_axis=4, concat_axis=2, tiled=True)[0, 0]]
    convert_element_type x6 -> x0, other arithmetic: 5.92 us -> none  [head_grads(): score_grad = (probs * (prob_grad - row_dot)).astype(jnp.bfloat16)]
    another operation x1 -> x0, local copies, waits for them, and re-layouts: 5.76 us -> none  [attend(): jnp.stack([join_heads(query_grad), join_heads(key_grad), join_heads(value...]
  transfers between devices with their start and end apart: 3 -> 0, of which waited for: 2 -> 0; matrix products, arithmetic and copies ran while one was open for 12% -> 0% of each run, Pallas kernels for 0% -> 0%
where the time goes in v1:
time: 108 us
  Pallas kernels  102 us (94%)
  local copies, waits for them, and re-layouts  4.4 us (4%)
  between operations  1.94 us (2%)
    pallas_call x1, Pallas kernels, body(): pl.pallas_call(functools.partial(kernel, dp, seq, branch, chunks, tokens)...  102 us
    unnamed x4, local copies, waits for them, and re-layouts  4.4 us

profile of v1, /device:TPU:0, one launch (start us, length us, event | category | flops | bytes accessed | tf_op | source)
XLA Modules:
  0.0 108.2 jit_solution(17101402686156725375)
XLA Ops:
  1.9 101.9 %shard_map.68 = (bf16[3,224,1536]{2,1,0:T(8,128)(2,1)}, f32[1216,384]{1,0:T(8,128)}) custom-call(bf16[3,224,1536]{2,1,0:T(8,128)(2,1)} %bitcast.9, bf16[56,2432]{1,0:T(8,128)(2,1)} %bitcast.13, bf16[384,2432]{1,0:T(8,128)(2,1)} %bitcast.12, s32[1]{0:T(128)S(6)} %copy.9.level_ref, s32[1]{0:T(128)S(6)} %copy.10.count_ref), custom_call_target="tpu_custom_call" | custom-call | tf_op jit(solution)/shard_map/pallas_call | solution.py:266
  103.8 0.0 copy-start
  103.9 3.2 %copy.11 = bf16[1,1,224,3,1536]{4,2,3,1,0:T(8,128)(2,1)} copy(bf16[1,1,224,3,1536]{4,2,3,1,0:T(8,128)(2,1)} %bitcast.10) | data formatting | bytes 4128768
  107.0 0.0 copy-done
  107.0 1.2 %copy.12 = f32[1,1216,384]{2,1,0:T(8,128)} copy(f32[1,1216,384]{2,1,0:T(8,128)S(1)} %bitcast.11) | data formatting | bytes 3735552
Async XLA Ops:
  103.8 3.2 %copy-start = (f32[1216,384]{1,0:T(8,128)S(1)}, f32[1216,384]{1,0:T(8,128)}, u32[]{:S(2)}) copy-start(f32[1216,384]{1,0:T(8,128)} %get-tuple-element.5) | copy-start | bytes 5603332

commit v2 on v1

--- a/solution.py
+++ b/solution.py
@@ -32,7 +32,7 @@
     dp, seq, branch, chunks, tokens,
     x_ref, gb_ref, w_ref, level_ref, count_ref,
     out_ref, wg_ref,
-    inb, slots, upc, dot_s, e_s, att32, inv_s, attb, q_t, k_t, v_t, gbuf, acc, partf, part_b, rbuf,
+    inb, slots, up, up_t, grad_s, dot_s, e_s, att32, inv_s, q_t, k_t, v_t, gbuf, acc, partf, part_b, rbuf,
     qs, qr, rs, rr, zs, zr, ys, yr, cs, cr, fs, fr, ds_, dr, own_q, own_r,
 ):
     me_dp = lax.axis_index("dp")
@@ -53,12 +53,15 @@
         pl.semaphore_signal(barrier, inc=1, device_id={"dp": lax.rem(me_dp + d, dp)}, device_id_type=MESH)
 
     own = me_b * seq + me
-    rows = gb_ref.shape[0]
-    pad = slots.shape[1]
-    mine = jnp.concatenate(
-        [gb_ref[...].astype(F32), jnp.zeros((pad - rows, gb_ref.shape[1]), F32)], axis=0
-    ).astype(BF16)
-    slots[own] = mine
+    rows, model = gb_ref.shape
+    full = rows // 16
+    half = (slots.shape[2] - full * model)
+    last = gb_ref[...].astype(F32)[full * 16:]
+    filler = jnp.zeros((8, 2 * half - model), F32)
+    last = jnp.concatenate([last[:, :half], jnp.concatenate([last[:, half:], filler], axis=1)], axis=0)
+    for i in range(full):
+        slots[own, :, i * model:(i + 1) * model] = gb_ref[i * 16:(i + 1) * 16, :]
+    slots[own, :, full * model:] = last.astype(BF16)
     pl.semaphore_wait(barrier, branch + seq + dp - 3)
 
     def remote(src, dst, ssem, rsem, axis, index):
@@ -105,8 +108,9 @@
         at = pl.ds(pl.multiple_of(me * part, 16), part)
         return pltpu.make_async_copy(gbuf.at[c, :, at, :], out_ref.at[:, :, lanes], own_r.at[c])
 
-    def dp_copy(d):
-        return remote(part_b.at[d - 1], rbuf.at[d - 1], ds_.at[d - 1], dr.at[d - 1], "dp", lax.rem(me_dp + d, dp))
+    def dp_copy(c, d):
+        to = lax.rem(me_dp + d, dp)
+        return remote(part_b.at[d - 1, c], rbuf.at[d - 1, c], ds_.at[d - 1, c], dr.at[d - 1, c], "dp", to)
 
     def send_qkv(c):
         for d in (2, 1, 3):
@@ -118,8 +122,6 @@
     send_qkv(0)
     y_copy(0).start()
     c_copy(0).start()
-    send_qkv(1)
-    send_qkv(2)
 
     level = level_ref[0]
     limit = LAT + count_ref[0]
@@ -131,6 +133,8 @@
         for d in range(1, seq):
             qkv_copy(c, d).wait_recv()
         qkv_own(c).wait()
+        if 0 < c < chunks - 1:
+            send_qkv(c + 1)
         q_t[c] = (inb[c, 0].astype(F32) * 0.125).T.astype(BF16)
         k_t[c] = inb[c, 1].astype(F32).T.astype(BF16)
         v_t[c] = inb[c, 2].astype(F32).T.astype(BF16)
@@ -147,7 +151,6 @@
             e_s[c, :, wide] = eb
             o = fold_diag(jnp.dot(v_t[c], eb, preferred_element_type=F32) * inv)
             att32[c, :, lanes] = o
-            attb[pl.ds(c * W, W), lanes] = o.astype(BF16)
             inv_s[c, :, lanes] = fold_diag(jnp.broadcast_to(inv, (W, 2 * W)))
             return carry
 
@@ -155,11 +158,12 @@
 
     def backward(c):
         acc[...] = jnp.zeros_like(acc)
+        dot_s[...] = grad_s[:, c * W:(c + 1) * W].T
 
         def step(i, carry):
             lanes = pl.ds(pl.multiple_of(i * W, W), W)
             wide = pl.ds(pl.multiple_of(i * 2 * W, 2 * W), 2 * W)
-            do = (dot_s[pl.ds(c * W, W), lanes] * inv_s[c, :, lanes]).astype(BF16)
+            do = (dot_s[:, lanes] * inv_s[c, :, lanes]).astype(BF16)
             prod = do.astype(F32) * att32[c, :, lanes]
             delta = jnp.concatenate(
                 [jnp.sum(prod[:64], axis=0, keepdims=True), jnp.sum(prod[64:], axis=0, keepdims=True)], axis=1
@@ -186,53 +190,72 @@
         y_copy(d).start()
         c_copy(d).start()
 
+    def quarter(d):
+        c_copy(d).wait_recv()
+        f_copy(d).wait_recv()
+        b = lax.rem(me_b - d + branch, branch)
+        pieces = []
+        for j in range(seq):
+            block = slots[b * seq + j].astype(F32)
+            pieces += [block[:, i * model:(i + 1) * model] for i in range(full)]
+            rest = block[:, full * model:]
+            pieces.append(jnp.concatenate([rest[:8], rest[8:, :model - half]], axis=1))
+        pieces.append(jnp.zeros((up.shape[1] - part, model), F32))
+        up[b] = jnp.concatenate(pieces, axis=0).astype(BF16)
+        at = pl.ds(pl.multiple_of(b * part, 16), part)
+        grad_s[at, :] = factor * lax.dot_general(up[b, :part, :], w_ref[...], NT, preferred_element_type=F32)
+
+    def turn(d):
+        b = lax.rem(me_b - d + branch, branch)
+        up_t[b] = up[b].T
+
+    def weight(c):
+        att = att32[c].astype(BF16)
+        fill = jnp.zeros((W, up.shape[1] - part), BF16)
+        sum_ = jnp.zeros((model, W), F32)
+        for b in range(branch):
+            att_b = jnp.concatenate([att[:, b * part:(b + 1) * part], fill], axis=1)
+            sum_ = sum_ + lax.dot_general(up_t[b], att_b, NT, preferred_element_type=F32)
+        partf[c] = sum_ * factor
+        for d in range(1, dp):
+            to = lax.rem(me_dp + d, dp)
+            part_b[d - 1, c] = partf[c, pl.ds(pl.multiple_of(to * share, 8), share), :].astype(BF16)
+            dp_copy(c, d).start()
+
+    share = wg_ref.shape[0]
     forward(0)
-    for d in range(1, branch):
-        relay(d)
     y_copy(0).wait_recv()
     f_copy(0).start()
-    forward(1)
-    for d in range(1, branch):
+    relay(1)
+    quarter(0)
+    relay(2)
+    y_copy(1).wait_recv()
+    f_copy(1).start()
+    relay(3)
+    send_qkv(1)
+    turn(0)
+    quarter(1)
+    turn(1)
+    for d in range(2, branch):
         y_copy(d).wait_recv()
         f_copy(d).start()
-    forward(2)
-    for d in range(branch):
-        c_copy(d).wait_recv()
-        f_copy(d).wait_recv()
-
-    for b in range(branch):
-        whole = jnp.concatenate([slots[b * seq + j].astype(F32)[:rows] for j in range(seq)], axis=0)
-        upc[b * seq * rows:(b + 1) * seq * rows, :] = whole.astype(BF16)
-
-    for at in range(0, tokens, 2 * W):
-        size = min(2 * W, tokens - at)
-        dot_s[:, at:at + size] = factor * lax.dot_general(
-            w_ref[...], upc[at:at + size, :], NT, preferred_element_type=F32
-        )
-
+        quarter(d)
+        if d < branch - 1:
+            turn(d)
     backward(0)
-
-    def weight_step(j, carry):
-        lanes = pl.ds(pl.multiple_of(j * W, W), W)
-        r = jnp.dot(attb[...], upc[:, lanes], preferred_element_type=F32)
-        partf[lanes, :] = r.T * factor
-        return carry
-
-    lax.fori_loop(0, upc.shape[1] // W, weight_step, 0)
-    share = wg_ref.shape[0]
-    for d in range(1, dp):
-        to = lax.rem(me_dp + d, dp)
-        part_b[d - 1] = partf[pl.ds(pl.multiple_of(to * share, 8), share), :].astype(BF16)
-        dp_copy(d).start()
-
+    turn(branch - 1)
+    weight(0)
     for c in range(1, chunks):
+        forward(c)
         backward(c)
-
-    total = partf[pl.ds(pl.multiple_of(me_dp * share, 8), share), :]
-    for d in range(1, dp):
-        dp_copy(d).wait_recv()
-        total = total + rbuf[d - 1].astype(F32)
-    wg_ref[...] = total
+        weight(c)
+
+    for c in range(chunks):
+        total = partf[c, pl.ds(pl.multiple_of(me_dp * share, 8), share), :]
+        for d in range(1, dp):
+            dp_copy(c, d).wait_recv()
+            total = total + rbuf[d - 1, c].astype(F32)
+        wg_ref[:, c * W:(c + 1) * W] = total
 
     for c in range(chunks):
         ret_own(c).wait()
@@ -247,7 +270,8 @@
         c_copy(d).wait_send()
         f_copy(d).wait_send()
     for d in range(1, dp):
-        dp_copy(d).wait_send()
+        for c in range(chunks):
+            dp_copy(c, d).wait_send()
 
 
 def body(dp, seq, branch, qkv, grad_base, w_out, scale_level, text_count):
@@ -256,7 +280,9 @@
     width = features // seq
     chunks = width // W
     rows, model = grad_base.shape[1:]
-    pad = -(-rows // 16) * 16
+    tiles = rows // 8 * (model // W)
+    packed = (tiles + tiles % 2) // 2 * W
+    group = -(-part // W) * W
     share = model // dp
     dma = pltpu.SemaphoreType.DMA
     vm = pltpu.VMEM
@@ -273,28 +299,29 @@
         out_specs=(anyspec, vspec),
         scratch_shapes=[
             vm((chunks, 3, tokens, W), BF16),
-            vm((branch * seq, pad, model), BF16),
-            vm((tokens, model), BF16),
-            vm((width, tokens), F32),
+            vm((branch * seq, 16, packed), BF16),
+            vm((branch, group, model), BF16),
+            vm((branch, model, group), BF16),
+            vm((tokens, width), F32),
+            vm((W, tokens), F32),
             vm((chunks, tokens, 2 * tokens), BF16),
             vm((chunks, W, tokens), F32),
             vm((chunks, W, tokens), F32),
-            vm((width, tokens), BF16),
             vm((chunks, W, tokens), BF16),
             vm((chunks, W, tokens), BF16),
             vm((chunks, W, tokens), BF16),
             vm((chunks, 3, tokens, W), BF16),
             vm((2, tokens, W), F32),
-            vm((model, width), F32),
-            vm((dp - 1, share, width), BF16),
-            vm((dp - 1, share, width), BF16),
+            vm((chunks, model, W), F32),
+            vm((dp - 1, chunks, share, W), BF16),
+            vm((dp - 1, chunks, share, W), BF16),
             dma((chunks, seq - 1)), dma((chunks, seq - 1)),
             dma((chunks, seq - 1)), dma((chunks, seq - 1)),
             dma((branch - 1,)), dma((branch - 1,)),
             dma((branch,)), dma((branch,)),
             dma((branch,)), dma((branch,)),
             dma((branch,)), dma((branch,)),
-            dma((dp - 1,)), dma((dp - 1,)),
+            dma((dp - 1, chunks)), dma((dp - 1, chunks)),
             dma((chunks,)), dma((chunks,)),
         ],
         compiler_params=pltpu.CompilerParams(

time: 108 us -> 94.6 us (0.88)
  Pallas kernels: 102 us -> 87.9 us
    pallas_call x1, Pallas kernels: 102 us -> 87.9 us  [body(): pl.pallas_call(functools.partial(kernel, dp, seq, branch, chunks, tokens)...]
where the time goes in v2:
time: 94.6 us; the launch traced here: 94.2 us
  Pallas kernels  87.9 us (93%)
  local copies, waits for them, and re-layouts  4.4 us (5%)
  between operations  1.94 us (2%)
    pallas_call x1, Pallas kernels, body(): pl.pallas_call(functools.partial(kernel, dp, seq, branch, chunks, tokens)...  87.9 us
    unnamed x4, local copies, waits for them, and re-layouts  4.4 us

profile of v2, /device:TPU:0, one launch (start us, length us, event | category | flops | bytes accessed | tf_op | source)
XLA Modules:
  0.0 94.2 jit_solution(1211847965973128557)
XLA Ops:
  1.9 87.9 %shard_map.68 = (bf16[3,224,1536]{2,1,0:T(8,128)(2,1)}, f32[1216,384]{1,0:T(8,128)}) custom-call(bf16[3,224,1536]{2,1,0:T(8,128)(2,1)} %bitcast.9, bf16[56,2432]{1,0:T(8,128)(2,1)} %bitcast.13, bf16[384,2432]{1,0:T(8,128)(2,1)} %bitcast.12, s32[1]{0:T(128)S(6)} %copy.9.level_ref, s32[1]{0:T(128)S(6)} %copy.10.count_ref), custom_call_target="tpu_custom_call" | custom-call | tf_op jit(solution)/shard_map/pallas_call | solution.py:292
  89.8 0.0 copy-start
  89.8 3.2 %copy.11 = bf16[1,1,224,3,1536]{4,2,3,1,0:T(8,128)(2,1)} copy(bf16[1,1,224,3,1536]{4,2,3,1,0:T(8,128)(2,1)} %bitcast.10) | data formatting | bytes 4128768
  92.9 0.0 copy-done
  93.0 1.2 %copy.12 = f32[1,1216,384]{2,1,0:T(8,128)} copy(f32[1,1216,384]{2,1,0:T(8,128)S(1)} %bitcast.11) | data formatting | bytes 3735552
Async XLA Ops:
  89.8 3.2 %copy-start = (f32[1216,384]{1,0:T(8,128)S(1)}, f32[1216,384]{1,0:T(8,128)}, u32[]{:S(2)}) copy-start(f32[1216,384]{1,0:T(8,128)} %get-tuple-element.5) | copy-start | bytes 5603332

commit v3 on v2

--- a/solution.py
+++ b/solution.py
@@ -32,7 +32,7 @@
     dp, seq, branch, chunks, tokens,
     x_ref, gb_ref, w_ref, level_ref, count_ref,
     out_ref, wg_ref,
-    inb, slots, up, up_t, grad_s, dot_s, e_s, att32, inv_s, q_t, k_t, v_t, gbuf, acc, partf, part_b, rbuf,
+    inb, slots, up, up_t, grad_s, do_t, att_t, q_t, k_t, v_t, gbuf, acc, partf, part_b, rbuf,
     qs, qr, rs, rr, zs, zr, ys, yr, cs, cr, fs, fr, ds_, dr, own_q, own_r,
 ):
     me_dp = lax.axis_index("dp")
@@ -117,11 +117,11 @@
             qkv_copy(c, d).start()
         qkv_own(c).start()
 
-    for d in range(1, branch):
-        z_copy(d).start()
-    send_qkv(0)
+    z_copy(1).start()
+    z_copy(branch - 1).start()
     y_copy(0).start()
     c_copy(0).start()
+    send_qkv(0)
 
     level = level_ref[0]
     limit = LAT + count_ref[0]
@@ -129,56 +129,44 @@
     safe = LAT + MIN_TEXT
     tail = safe + lax.broadcasted_iota(jnp.int32, (tokens - safe, 2 * W), 0)
 
-    def forward(c):
+    def attention(c):
         for d in range(1, seq):
             qkv_copy(c, d).wait_recv()
         qkv_own(c).wait()
-        if 0 < c < chunks - 1:
-            send_qkv(c + 1)
-        q_t[c] = (inb[c, 0].astype(F32) * 0.125).T.astype(BF16)
-        k_t[c] = inb[c, 1].astype(F32).T.astype(BF16)
-        v_t[c] = inb[c, 2].astype(F32).T.astype(BF16)
-
-        def step(i, carry):
-            lanes = pl.ds(pl.multiple_of(i * W, W), W)
-            wide = pl.ds(pl.multiple_of(i * 2 * W, 2 * W), 2 * W)
-            s = jnp.dot(inb[c, 1], block_diag(q_t[c, :, lanes]), preferred_element_type=F32)
+
+        @pl.when(c + 2 < chunks)
+        def _():
+            send_qkv(c + 2)
+
+        q_t[...] = (inb[c, 0].astype(F32) * 0.125).T.astype(BF16)
+        k_t[...] = inb[c, 1].astype(F32).T.astype(BF16)
+        v_t[...] = inb[c, 2].astype(F32).T.astype(BF16)
+        do_t[...] = grad_s[:, pl.ds(pl.multiple_of(c * W, W), W)].T.astype(BF16)
+        acc[...] = jnp.zeros_like(acc)
+
+        for i in range(nblk):
+            lanes = slice(i * W, (i + 1) * W)
+            do = do_t[:, lanes]
+            bdq = block_diag(q_t[:, lanes])
+            bdo = block_diag(do)
+            s = jnp.dot(inb[c, 1], bdq, preferred_element_type=F32)
+            dpr = jnp.dot(inb[c, 2], bdo, preferred_element_type=F32)
             s = jnp.concatenate([s[:safe], jnp.where(tail < limit, s[safe:], -1e30)], axis=0)
-            top = jnp.max(s, axis=0, keepdims=True)
-            e = jnp.exp(s - top)
-            inv = 1.0 / jnp.sum(e, axis=0, keepdims=True)
-            eb = e.astype(BF16)
-            e_s[c, :, wide] = eb
-            o = fold_diag(jnp.dot(v_t[c], eb, preferred_element_type=F32) * inv)
-            att32[c, :, lanes] = o
-            inv_s[c, :, lanes] = fold_diag(jnp.broadcast_to(inv, (W, 2 * W)))
-            return carry
-
-        lax.fori_loop(0, nblk, step, 0)
-
-    def backward(c):
-        acc[...] = jnp.zeros_like(acc)
-        dot_s[...] = grad_s[:, c * W:(c + 1) * W].T
-
-        def step(i, carry):
-            lanes = pl.ds(pl.multiple_of(i * W, W), W)
-            wide = pl.ds(pl.multiple_of(i * 2 * W, 2 * W), 2 * W)
-            do = (dot_s[:, lanes] * inv_s[c, :, lanes]).astype(BF16)
-            prod = do.astype(F32) * att32[c, :, lanes]
+            e = jnp.exp(s - jnp.max(s, axis=0, keepdims=True))
+            probs = e * (1.0 / jnp.sum(e, axis=0, keepdims=True))
+            pb = probs.astype(BF16)
+            o = fold_diag(jnp.dot(v_t[...], pb, preferred_element_type=F32))
+            att_t[c, :, lanes] = o.astype(BF16)
+            prod = do.astype(F32) * o
             delta = jnp.concatenate(
                 [jnp.sum(prod[:64], axis=0, keepdims=True), jnp.sum(prod[64:], axis=0, keepdims=True)], axis=1
             )
-            bd = block_diag(do)
-            dpr = jnp.dot(inb[c, 2], bd, preferred_element_type=F32)
-            eb = e_s[c, :, wide]
-            ds = (eb.astype(F32) * (dpr - delta)).astype(BF16)
-            acc[1] += lax.dot_general(eb, bd, NT, preferred_element_type=F32)
-            acc[0] += lax.dot_general(ds, block_diag(q_t[c, :, lanes]), NT, preferred_element_type=F32)
-            dq = fold_diag(jnp.dot(k_t[c], ds, preferred_element_type=F32)) * 0.125
+            acc[1] += lax.dot_general(pb, bdo, NT, preferred_element_type=F32)
+            ds = (probs * (dpr - delta)).astype(BF16)
+            acc[0] += lax.dot_general(ds, bdq, NT, preferred_element_type=F32)
+            dq = fold_diag(jnp.dot(k_t[...], ds, preferred_element_type=F32)) * 0.125
             gbuf[c, 0, lanes, :] = dq.T.astype(BF16)
-            return carry
-
-        lax.fori_loop(0, nblk, step, 0)
+
         gbuf[c, 1] = acc[0].astype(BF16)
         gbuf[c, 2] = acc[1].astype(BF16)
         for d in (2, 1, 3):
@@ -210,7 +198,7 @@
         up_t[b] = up[b].T
 
     def weight(c):
-        att = att32[c].astype(BF16)
+        att = att_t[c]
         fill = jnp.zeros((W, up.shape[1] - part), BF16)
         sum_ = jnp.zeros((model, W), F32)
         for b in range(branch):
@@ -223,32 +211,34 @@
             dp_copy(c, d).start()
 
     share = wg_ref.shape[0]
-    forward(0)
+    far = [d for d in range(2, branch - 1)]
+    relay(1)
+    for d in far:
+        z_copy(d).start()
     y_copy(0).wait_recv()
     f_copy(0).start()
-    relay(1)
+    relay(branch - 1)
     quarter(0)
-    relay(2)
+    turn(0)
     y_copy(1).wait_recv()
     f_copy(1).start()
-    relay(3)
-    send_qkv(1)
-    turn(0)
     quarter(1)
     turn(1)
-    for d in range(2, branch):
+    for d in far:
+        relay(d)
+    send_qkv(1)
+    for d in [branch - 1] + far:
         y_copy(d).wait_recv()
         f_copy(d).start()
         quarter(d)
-        if d < branch - 1:
-            turn(d)
-    backward(0)
-    turn(branch - 1)
-    weight(0)
-    for c in range(1, chunks):
-        forward(c)
-        backward(c)
+        turn(d)
+
+    def head_pair(c, carry):
+        attention(c)
         weight(c)
+        return carry
+
+    lax.fori_loop(0, chunks, head_pair, 0)
 
     for c in range(chunks):
         total = partf[c, pl.ds(pl.multiple_of(me_dp * share, 8), share), :]
@@ -303,13 +293,11 @@
             vm((branch, group, model), BF16),
             vm((branch, model, group), BF16),
             vm((tokens, width), F32),
-            vm((W, tokens), F32),
-            vm((chunks, tokens, 2 * tokens), BF16),
-            vm((chunks, W, tokens), F32),
-            vm((chunks, W, tokens), F32),
+            vm((W, tokens), BF16),
             vm((chunks, W, tokens), BF16),
-            vm((chunks, W, tokens), BF16),
-            vm((chunks, W, tokens), BF16),
+            vm((W, tokens), BF16),
+            vm((W, tokens), BF16),
+            vm((W, tokens), BF16),
             vm((chunks, 3, tokens, W), BF16),
             vm((2, tokens, W), F32),
             vm((chunks, model, W), F32),

time: 94.6 us -> 89.7 us (0.948)
  Pallas kernels: 87.9 us -> 83 us
    pallas_call x1, Pallas kernels: 87.9 us -> 83 us  [body(): pl.pallas_call(functools.partial(kernel, dp, seq, branch, chunks, tokens)...]
where the time goes in v3:
time: 89.7 us; the launch traced here: 89.3 us
  Pallas kernels  83 us (93%)
  local copies, waits for them, and re-layouts  4.4 us (5%)
  between operations  1.94 us (2%)
    pallas_call x1, Pallas kernels, body(): pl.pallas_call(functools.partial(kernel, dp, seq, branch, chunks, tokens)...  83 us
    unnamed x4, local copies, waits for them, and re-layouts  4.4 us

profile of v3, /device:TPU:0, one launch (start us, length us, event | category | flops | bytes accessed | tf_op | source)
XLA Modules:
  0.0 89.3 jit_solution(8181722123212729185)
XLA Ops:
  1.9 83.0 %shard_map.68 = (bf16[3,224,1536]{2,1,0:T(8,128)(2,1)}, f32[1216,384]{1,0:T(8,128)}) custom-call(bf16[3,224,1536]{2,1,0:T(8,128)(2,1)} %bitcast.9, bf16[56,2432]{1,0:T(8,128)(2,1)} %bitcast.13, bf16[384,2432]{1,0:T(8,128)(2,1)} %bitcast.12, s32[1]{0:T(128)S(6)} %copy.9.level_ref, s32[1]{0:T(128)S(6)} %copy.10.count_ref), custom_call_target="tpu_custom_call" | custom-call | tf_op jit(solution)/shard_map/pallas_call | solution.py:282
  84.9 0.0 copy-start
  84.9 3.2 %copy.11 = bf16[1,1,224,3,1536]{4,2,3,1,0:T(8,128)(2,1)} copy(bf16[1,1,224,3,1536]{4,2,3,1,0:T(8,128)(2,1)} %bitcast.10) | data formatting | bytes 4128768
  88.1 0.0 copy-done
  88.1 1.2 %copy.12 = f32[1,1216,384]{2,1,0:T(8,128)} copy(f32[1,1216,384]{2,1,0:T(8,128)S(1)} %bitcast.11) | data formatting | bytes 3735552
Async XLA Ops:
  84.9 3.2 %copy-start = (f32[1216,384]{1,0:T(8,128)S(1)}, f32[1216,384]{1,0:T(8,128)}, u32[]{:S(2)}) copy-start(f32[1216,384]{1,0:T(8,128)} %get-tuple-element.5) | copy-start | bytes 5603332

commit v4 on v3

--- a/solution.py
+++ b/solution.py
@@ -33,7 +33,7 @@
     x_ref, gb_ref, w_ref, level_ref, count_ref,
     out_ref, wg_ref,
     inb, slots, up, up_t, grad_s, do_t, att_t, q_t, k_t, v_t, gbuf, acc, partf, part_b, rbuf,
-    qs, qr, rs, rr, zs, zr, ys, yr, cs, cr, fs, fr, ds_, dr, own_q, own_r,
+    qs, qr, rs, rr, zs, zr, bs, br, ys, yr, cs, cr, fs, fr, ds_, dr, own_q, own_r,
 ):
     me_dp = lax.axis_index("dp")
     me_b = lax.axis_index("branch")
@@ -84,11 +84,28 @@
     def line(d):
         return lax.rem(me_b - d + branch, branch) * seq + me
 
+    cut = slots.shape[2] // W // 2 * W
+    first, second = slice(0, cut), slice(cut, slots.shape[2])
+
+    def on_line(d):
+        if d in (1, branch - 1):
+            return 0, lax.rem(me_b + d, branch)
+        return d - 1, lax.rem(me_b + 1, branch)
+
     def z_copy(d):
-        return remote(slots.at[own], slots.at[own], zs.at[d - 1], zr.at[d - 1], "branch", lax.rem(me_b + d, branch))
+        back, to = on_line(d)
+        block = slots.at[line(back)]
+        return remote(block, block, zs.at[d - 1], zr.at[d - 1], "branch", to)
+
+    def b_copy(d):
+        back, to = on_line(d)
+        k = lax.rem(me_b - back + branch, branch) * seq + across
+        block = slots.at[k, :, second]
+        return remote(block, block, bs.at[d - 1], br.at[d - 1], "branch", to)
 
     def y_copy(d):
-        return remote(slots.at[line(d)], slots.at[line(d)], ys.at[d], yr.at[d], "seq", across)
+        block = slots.at[line(d)] if d == 0 else slots.at[line(d), :, first]
+        return remote(block, block, ys.at[d], yr.at[d], "seq", across)
 
     def c_copy(d):
         return remote(slots.at[line(d)], slots.at[line(d)], cs.at[d], cr.at[d], "seq", beside)
@@ -195,15 +212,17 @@
 
     def turn(d):
         b = lax.rem(me_b - d + branch, branch)
-        up_t[b] = up[b].T
+        group = up.shape[1]
+        up_t[:, pl.ds(pl.multiple_of(b * group, W), group)] = up[b].T
 
     def weight(c):
         att = att_t[c]
         fill = jnp.zeros((W, up.shape[1] - part), BF16)
-        sum_ = jnp.zeros((model, W), F32)
+        pieces = []
         for b in range(branch):
-            att_b = jnp.concatenate([att[:, b * part:(b + 1) * part], fill], axis=1)
-            sum_ = sum_ + lax.dot_general(up_t[b], att_b, NT, preferred_element_type=F32)
+            pieces += [att[:, b * part:(b + 1) * part], fill]
+        att = jnp.concatenate(pieces, axis=1)
+        sum_ = lax.dot_general(up_t[...], att, NT, preferred_element_type=F32)
         partf[c] = sum_ * factor
         for d in range(1, dp):
             to = lax.rem(me_dp + d, dp)
@@ -211,27 +230,34 @@
             dp_copy(c, d).start()
 
     share = wg_ref.shape[0]
-    far = [d for d in range(2, branch - 1)]
-    relay(1)
-    for d in far:
-        z_copy(d).start()
+    def cross(d):
+        y_copy(d).wait_recv()
+        f_copy(d).start()
+
     y_copy(0).wait_recv()
     f_copy(0).start()
+    b_copy(1).start()
+    b_copy(branch - 1).start()
+    relay(1)
+    z_copy(2).start()
     relay(branch - 1)
+    b_copy(1).wait_recv()
+    b_copy(2).start()
     quarter(0)
     turn(0)
-    y_copy(1).wait_recv()
-    f_copy(1).start()
+    cross(1)
+    relay(2)
+    send_qkv(1)
+    b_copy(branch - 1).wait_recv()
+    cross(branch - 1)
     quarter(1)
     turn(1)
-    for d in far:
-        relay(d)
-    send_qkv(1)
-    for d in [branch - 1] + far:
-        y_copy(d).wait_recv()
-        f_copy(d).start()
-        quarter(d)
-        turn(d)
+    b_copy(2).wait_recv()
+    cross(2)
+    quarter(branch - 1)
+    turn(branch - 1)
+    quarter(2)
+    turn(2)
 
     def head_pair(c, carry):
         attention(c)
@@ -255,6 +281,7 @@
             qkv_copy(c, d).wait_send()
     for d in range(1, branch):
         z_copy(d).wait_send()
+        b_copy(d).wait_send()
     for d in range(branch):
         y_copy(d).wait_send()
         c_copy(d).wait_send()
@@ -291,7 +318,7 @@
             vm((chunks, 3, tokens, W), BF16),
             vm((branch * seq, 16, packed), BF16),
             vm((branch, group, model), BF16),
-            vm((branch, model, group), BF16),
+            vm((model, branch * group), BF16),
             vm((tokens, width), F32),
             vm((W, tokens), BF16),
             vm((chunks, W, tokens), BF16),
@@ -306,6 +333,7 @@
             dma((chunks, seq - 1)), dma((chunks, seq - 1)),
             dma((chunks, seq - 1)), dma((chunks, seq - 1)),
             dma((branch - 1,)), dma((branch - 1,)),
+            dma((branch - 1,)), dma((branch - 1,)),
             dma((branch,)), dma((branch,)),
             dma((branch,)), dma((branch,)),
             dma((branch,)), dma((branch,)),

time: 89.7 us -> 89.5 us (level)
  no operation moved by 1% of the time
where the time goes in v4:
time: 89.5 us; the launch traced here: 89.3 us
  Pallas kernels  83 us (93%)
  local copies, waits for them, and re-layouts  4.4 us (5%)
  between operations  1.94 us (2%)
    pallas_call x1, Pallas kernels, body(): pl.pallas_call(functools.partial(kernel, dp, seq, branch, chunks, tokens)...  83 us
    unnamed x4, local copies, waits for them, and re-layouts  4.4 us

profile of v4, /device:TPU:0, one launch (start us, length us, event | category | flops | bytes accessed | tf_op | source)
XLA Modules:
  0.0 89.3 jit_solution(11777175719907606849)
XLA Ops:
  1.9 83.0 %shard_map.68 = (bf16[3,224,1536]{2,1,0:T(8,128)(2,1)}, f32[1216,384]{1,0:T(8,128)}) custom-call(bf16[3,224,1536]{2,1,0:T(8,128)(2,1)} %bitcast.9, bf16[56,2432]{1,0:T(8,128)(2,1)} %bitcast.13, bf16[384,2432]{1,0:T(8,128)(2,1)} %bitcast.12, s32[1]{0:T(128)S(6)} %copy.9.level_ref, s32[1]{0:T(128)S(6)} %copy.10.count_ref), custom_call_target="tpu_custom_call" | custom-call | tf_op jit(solution)/shard_map/pallas_call | solution.py:309
  84.9 0.0 copy-start
  84.9 3.2 %copy.11 = bf16[1,1,224,3,1536]{4,2,3,1,0:T(8,128)(2,1)} copy(bf16[1,1,224,3,1536]{4,2,3,1,0:T(8,128)(2,1)} %bitcast.10) | data formatting | bytes 4128768
  88.0 0.0 copy-done
  88.1 1.2 %copy.12 = f32[1,1216,384]{2,1,0:T(8,128)} copy(f32[1,1216,384]{2,1,0:T(8,128)S(1)} %bitcast.11) | data formatting | bytes 3735552
Async XLA Ops:
  84.9 3.2 %copy-start = (f32[1216,384]{1,0:T(8,128)S(1)}, f32[1216,384]{1,0:T(8,128)}, u32[]{:S(2)}) copy-start(f32[1216,384]{1,0:T(8,128)} %get-tuple-element.5) | copy-start | bytes 5603332

commit v5 on v4

--- a/solution.py
+++ b/solution.py
@@ -32,7 +32,7 @@
     dp, seq, branch, chunks, tokens,
     x_ref, gb_ref, w_ref, level_ref, count_ref,
     out_ref, wg_ref,
-    inb, slots, up, up_t, grad_s, do_t, att_t, q_t, k_t, v_t, gbuf, acc, partf, part_b, rbuf,
+    inb, slots, up, up_t, grad_s, do_t, probs_s, o_s, q_t, k_t, v_t, gbuf, acc, partf, part_b, rbuf,
     qs, qr, rs, rr, zs, zr, bs, br, ys, yr, cs, cr, fs, fr, ds_, dr, own_q, own_r,
 ):
     me_dp = lax.axis_index("dp")
@@ -139,6 +139,7 @@
     y_copy(0).start()
     c_copy(0).start()
     send_qkv(0)
+    send_qkv(1)
 
     level = level_ref[0]
     limit = LAT + count_ref[0]
@@ -146,42 +147,44 @@
     safe = LAT + MIN_TEXT
     tail = safe + lax.broadcasted_iota(jnp.int32, (tokens - safe, 2 * W), 0)
 
-    def attention(c):
+    def forward(c):
         for d in range(1, seq):
             qkv_copy(c, d).wait_recv()
         qkv_own(c).wait()
-
-        @pl.when(c + 2 < chunks)
-        def _():
-            send_qkv(c + 2)
-
-        q_t[...] = (inb[c, 0].astype(F32) * 0.125).T.astype(BF16)
-        k_t[...] = inb[c, 1].astype(F32).T.astype(BF16)
-        v_t[...] = inb[c, 2].astype(F32).T.astype(BF16)
+        q_t[c] = (inb[c, 0].astype(F32) * 0.125).T.astype(BF16)
+        k_t[c] = inb[c, 1].astype(F32).T.astype(BF16)
+        v_t[c] = inb[c, 2].astype(F32).T.astype(BF16)
+
+        def step(i, carry):
+            lanes = pl.ds(pl.multiple_of(i * W, W), W)
+            wide = pl.ds(pl.multiple_of(i * 2 * W, 2 * W), 2 * W)
+            s = jnp.dot(inb[c, 1], block_diag(q_t[c, :, lanes]), preferred_element_type=F32)
+            s = jnp.concatenate([s[:safe], jnp.where(tail < limit, s[safe:], -1e30)], axis=0)
+            e = jnp.exp(s - jnp.max(s, axis=0, keepdims=True))
+            pb = (e * (1.0 / jnp.sum(e, axis=0, keepdims=True))).astype(BF16)
+            probs_s[c, :, wide] = pb
+            o_s[c, :, lanes] = fold_diag(jnp.dot(v_t[c], pb, preferred_element_type=F32))
+            return carry
+
+        lax.fori_loop(0, nblk, step, 0)
+
+    def backward(c):
         do_t[...] = grad_s[:, pl.ds(pl.multiple_of(c * W, W), W)].T.astype(BF16)
         acc[...] = jnp.zeros_like(acc)
-
         for i in range(nblk):
             lanes = slice(i * W, (i + 1) * W)
             do = do_t[:, lanes]
-            bdq = block_diag(q_t[:, lanes])
             bdo = block_diag(do)
-            s = jnp.dot(inb[c, 1], bdq, preferred_element_type=F32)
             dpr = jnp.dot(inb[c, 2], bdo, preferred_element_type=F32)
-            s = jnp.concatenate([s[:safe], jnp.where(tail < limit, s[safe:], -1e30)], axis=0)
-            e = jnp.exp(s - jnp.max(s, axis=0, keepdims=True))
-            probs = e * (1.0 / jnp.sum(e, axis=0, keepdims=True))
-            pb = probs.astype(BF16)
-            o = fold_diag(jnp.dot(v_t[...], pb, preferred_element_type=F32))
-            att_t[c, :, lanes] = o.astype(BF16)
-            prod = do.astype(F32) * o
+            prod = do.astype(F32) * o_s[c, :, lanes]
             delta = jnp.concatenate(
                 [jnp.sum(prod[:64], axis=0, keepdims=True), jnp.sum(prod[64:], axis=0, keepdims=True)], axis=1
             )
+            pb = probs_s[c, :, 2 * i * W:2 * (i + 1) * W]
             acc[1] += lax.dot_general(pb, bdo, NT, preferred_element_type=F32)
-            ds = (probs * (dpr - delta)).astype(BF16)
-            acc[0] += lax.dot_general(ds, bdq, NT, preferred_element_type=F32)
-            dq = fold_diag(jnp.dot(k_t[...], ds, preferred_element_type=F32)) * 0.125
+            ds = (pb.astype(F32) * (dpr - delta)).astype(BF16)
+            acc[0] += lax.dot_general(ds, block_diag(q_t[c, :, lanes]), NT, preferred_element_type=F32)
+            dq = fold_diag(jnp.dot(k_t[c], ds, preferred_element_type=F32)) * 0.125
             gbuf[c, 0, lanes, :] = dq.T.astype(BF16)
 
         gbuf[c, 1] = acc[0].astype(BF16)
@@ -216,7 +219,7 @@
         up_t[:, pl.ds(pl.multiple_of(b * group, W), group)] = up[b].T
 
     def weight(c):
-        att = att_t[c]
+        att = o_s[c].astype(BF16)
         fill = jnp.zeros((W, up.shape[1] - part), BF16)
         pieces = []
         for b in range(branch):
@@ -243,25 +246,30 @@
     relay(branch - 1)
     b_copy(1).wait_recv()
     b_copy(2).start()
+    forward(0)
+    cross(1)
+    relay(2)
+    for c in range(2, chunks):
+        send_qkv(c)
     quarter(0)
     turn(0)
-    cross(1)
-    relay(2)
-    send_qkv(1)
     b_copy(branch - 1).wait_recv()
     cross(branch - 1)
     quarter(1)
-    turn(1)
+    forward(1)
     b_copy(2).wait_recv()
     cross(2)
+    turn(1)
     quarter(branch - 1)
     turn(branch - 1)
+    for c in range(2, chunks):
+        forward(c)
     quarter(2)
     turn(2)
 
     def head_pair(c, carry):
-        attention(c)
         weight(c)
+        backward(c)
         return carry
 
     lax.fori_loop(0, chunks, head_pair, 0)
@@ -289,6 +297,20 @@
     for d in range(1, dp):
         for c in range(chunks):
             dp_copy(c, d).wait_send()
+
+
+def hand_over(grads_ref, weight_ref, grads_out, weight_out, grads_v, weight_v, in_sem, out_sem):
+    moves = [(grads_ref.at[i], grads_v.at[i], grads_out.at[i]) for i in range(3)]
+    moves.append((weight_ref, weight_v, weight_out))
+    loads = [pltpu.make_async_copy(a, v, in_sem.at[i]) for i, (a, v, _) in enumerate(moves)]
+    stores = [pltpu.make_async_copy(v, b, out_sem.at[i]) for i, (_, v, b) in enumerate(moves)]
+    for load in loads:
+        load.start()
+    for load, store in zip(loads, stores):
+        load.wait()
+        store.start()
+    for store in stores:
+        store.wait()
 
 
 def body(dp, seq, branch, qkv, grad_base, w_out, scale_level, text_count):
@@ -321,10 +343,11 @@
             vm((model, branch * group), BF16),
             vm((tokens, width), F32),
             vm((W, tokens), BF16),
+            vm((chunks, tokens, 2 * tokens), BF16),
+            vm((chunks, W, tokens), F32),
             vm((chunks, W, tokens), BF16),
-            vm((W, tokens), BF16),
-            vm((W, tokens), BF16),
-            vm((W, tokens), BF16),
+            vm((chunks, W, tokens), BF16),
+            vm((chunks, W, tokens), BF16),
             vm((chunks, 3, tokens, W), BF16),
             vm((2, tokens, W), F32),
             vm((chunks, model, W), F32),
@@ -344,6 +367,17 @@
             collective_id=0, has_side_effects=True, vmem_limit_bytes=58 * 1024 * 1024
         ),
     )(jnp.transpose(qkv[0, 0], (1, 0, 2)), grad_base[0], w_out[0], scale_level, text_count)
+    grads, weight_grad = pl.pallas_call(
+        hand_over,
+        out_shape=(
+            jax.ShapeDtypeStruct(grads.shape, BF16),
+            jax.ShapeDtypeStruct(weight_grad.shape, F32),
+        ),
+        in_specs=[anyspec, anyspec],
+        out_specs=(anyspec, anyspec),
+        scratch_shapes=[vm(grads.shape, BF16), vm(weight_grad.shape, F32), dma((4,)), dma((4,))],
+        compiler_params=pltpu.CompilerParams(vmem_limit_bytes=58 * 1024 * 1024),
+    )(grads, weight_grad)
     return (jnp.transpose(grads, (1, 0, 2))[None, None], weight_grad[None])
 
 

time: 89.5 us -> 90.4 us (1.010)
  Pallas kernels: 83 us -> 88.3 us
  local copies, waits for them, and re-layouts: 4.4 us -> 0 us
    unnamed x4 -> x0, local copies, waits for them, and re-layouts: 4.4 us -> none
    pallas_call x0 -> x1, Pallas kernels: none -> 3.62 us  [body(): pl.pallas_call(hand_over, out_shape=(jax.ShapeDtypeStruct(grads.shape, BF...]
    pallas_call x1, Pallas kernels: 83 us -> 84.7 us  [body(): pl.pallas_call(functools.partial(kernel, dp, seq, branch, chunks, tokens)...]
where the time goes in v5:
time: 90.4 us; the launch traced here: 90.3 us
  Pallas kernels  88.3 us (98%)
  between operations  1.93 us (2%)
    pallas_call x1, Pallas kernels, body(): pl.pallas_call(functools.partial(kernel, dp, seq, branch, chunks, tokens)...  84.7 us
    pallas_call x1, Pallas kernels, body(): pl.pallas_call(hand_over, out_shape=(jax.ShapeDtypeStruct(grads.shape, BF...  3.62 us

profile of v5, /device:TPU:0, one launch (start us, length us, event | category | flops | bytes accessed | tf_op | source)
XLA Modules:
  0.0 90.3 jit_solution(12285537056058166774)
XLA Ops:
  1.9 84.7 %shard_map.68 = (bf16[3,224,1536]{2,1,0:T(8,128)(2,1)}, f32[1216,384]{1,0:T(8,128)}) custom-call(bf16[3,224,1536]{2,1,0:T(8,128)(2,1)} %bitcast.9, bf16[56,2432]{1,0:T(8,128)(2,1)} %bitcast.11, bf16[384,2432]{1,0:T(8,128)(2,1)} %bitcast.10, s32[1]{0:T(128)S(6)} %copy.7.level_ref, s32[1]{0:T(128)S(6)} %copy.8.count_ref), custom_call_target="tpu_custom_call" | custom-call | tf_op jit(solution)/shard_map/pallas_call | solution.py:331
  86.7 3.6 %shard_map.69 = (bf16[3,224,1536]{2,1,0:T(8,128)(2,1)}, f32[1216,384]{1,0:T(8,128)}) custom-call(bf16[3,224,1536]{2,1,0:T(8,128)(2,1)} %get-tuple-element.6.grads_ref, f32[1216,384]{1,0:T(8,128)} %get-tuple-element.7.weight_ref), custom_call_target="tpu_custom_call" | custom-call | tf_op jit(solution)/shard_map/pallas_call | solution.py:370

commit v6 on v4

--- a/solution.py
+++ b/solution.py
@@ -289,6 +289,20 @@
     for d in range(1, dp):
         for c in range(chunks):
             dp_copy(c, d).wait_send()
+
+
+def hand_over(grads_ref, weight_ref, grads_out, weight_out, grads_v, weight_v, in_sem, out_sem):
+    moves = [(grads_ref.at[i], grads_v.at[i], grads_out.at[i]) for i in range(3)]
+    moves.append((weight_ref, weight_v, weight_out))
+    loads = [pltpu.make_async_copy(a, v, in_sem.at[i]) for i, (a, v, _) in enumerate(moves)]
+    stores = [pltpu.make_async_copy(v, b, out_sem.at[i]) for i, (_, v, b) in enumerate(moves)]
+    for load in loads:
+        load.start()
+    for load, store in zip(loads, stores):
+        load.wait()
+        store.start()
+    for store in stores:
+        store.wait()
 
 
 def body(dp, seq, branch, qkv, grad_base, w_out, scale_level, text_count):
@@ -344,6 +358,17 @@
             collective_id=0, has_side_effects=True, vmem_limit_bytes=58 * 1024 * 1024
         ),
     )(jnp.transpose(qkv[0, 0], (1, 0, 2)), grad_base[0], w_out[0], scale_level, text_count)
+    grads, weight_grad = pl.pallas_call(
+        hand_over,
+        out_shape=(
+            jax.ShapeDtypeStruct(grads.shape, BF16),
+            jax.ShapeDtypeStruct(weight_grad.shape, F32),
+        ),
+        in_specs=[anyspec, anyspec],
+        out_specs=(anyspec, anyspec),
+        scratch_shapes=[vm(grads.shape, BF16), vm(weight_grad.shape, F32), dma((4,)), dma((4,))],
+        compiler_params=pltpu.CompilerParams(vmem_limit_bytes=58 * 1024 * 1024),
+    )(grads, weight_grad)
     return (jnp.transpose(grads, (1, 0, 2))[None, None], weight_grad[None])
 
 

time: 89.5 us -> 88.8 us (level)
  local copies, waits for them, and re-layouts: 4.4 us -> 0 us
  Pallas kernels: 83 us -> 86.6 us
    unnamed x4 -> x0, local copies, waits for them, and re-layouts: 4.4 us -> none
    pallas_call x0 -> x1, Pallas kernels: none -> 3.62 us  [body(): pl.pallas_call(hand_over, out_shape=(jax.ShapeDtypeStruct(grads.shape, BF...]
where the time goes in v6:
time: 88.8 us; the launch traced here: 88.7 us
  Pallas kernels  86.6 us (98%)
  between operations  2.09 us (2%)
    pallas_call x1, Pallas kernels, body(): pl.pallas_call(functools.partial(kernel, dp, seq, branch, chunks, tokens)...  83 us
    pallas_call x1, Pallas kernels, body(): pl.pallas_call(hand_over, out_shape=(jax.ShapeDtypeStruct(grads.shape, BF...  3.62 us

profile of v6, /device:TPU:0, one launch (start us, length us, event | category | flops | bytes accessed | tf_op | source)
XLA Modules:
  0.0 88.7 jit_solution(3145054152645427428)
XLA Ops:
  1.9 83.0 %shard_map.68 = (bf16[3,224,1536]{2,1,0:T(8,128)(2,1)}, f32[1216,384]{1,0:T(8,128)}) custom-call(bf16[3,224,1536]{2,1,0:T(8,128)(2,1)} %bitcast.9, bf16[56,2432]{1,0:T(8,128)(2,1)} %bitcast.11, bf16[384,2432]{1,0:T(8,128)(2,1)} %bitcast.10, s32[1]{0:T(128)S(6)} %copy.7.level_ref, s32[1]{0:T(128)S(6)} %copy.8.count_ref), custom_call_target="tpu_custom_call" | custom-call | tf_op jit(solution)/shard_map/pallas_call | solution.py:323
  84.9 3.6 %shard_map.69 = (bf16[3,224,1536]{2,1,0:T(8,128)(2,1)}, f32[1216,384]{1,0:T(8,128)}) custom-call(bf16[3,224,1536]{2,1,0:T(8,128)(2,1)} %get-tuple-element.6.grads_ref, f32[1216,384]{1,0:T(8,128)} %get-tuple-element.7.weight_ref), custom_call_target="tpu_custom_call" | custom-call | tf_op jit(solution)/shard_map/pallas_call | solution.py:361
